TPU v7x, 32 devices: a whole 2x2x4 slice. The times are simulated.
32 devices in a mesh: dp: 8 (over y, x, core), table: 4 (over z).
Axes of the slice: x: 2, y: 2, z: 4, core: 2. Of those that a mesh axis runs over, the one named last changes fastest.
Arguments:
- knowledge: bfloat16 [5, 4608, 768], P(None, ('dp', 'table')), may hold values from -2.390625 to 2.390625
- expr_table: bfloat16 [128, 768], replicated, may hold values from -2.390625 to 2.390625
- gene_owner: int32 [8192, 1], P(('dp', 'table')), may hold values from 0 to 31; in each aligned block of 256 rows (0 to 255, 256 to 511, ...) at most 16 rows name the same one
- gene_row: int32 [8192], P(('dp', 'table')), may hold values from 0 to 143
- expr_bin: int32 [8192], P(('dp', 'table')), may hold values from 0 to 127
- cell_lengths: int32 [256], P(('dp', 'table')), may hold values from 0 to 256, as said below
- norm1_gain: float32 [768], replicated, may hold values from 0.5 to 1.5
- norm1_bias: float32 [768], replicated, may hold values from -1.8 to 1.8
- w_query: bfloat16 [768, 768], replicated, may hold values from -0.21875 to 0.21875
- b_query: float32 [768], replicated, may hold values from -1.8 to 1.8
- w_key: bfloat16 [768, 768], replicated, may hold values from -0.21875 to 0.21875
- w_value: bfloat16 [768, 768], replicated, may hold values from -0.21875 to 0.21875
- b_value: float32 [768], replicated, may hold values from -1.8 to 1.8
- w_attn_out: bfloat16 [768, 768], replicated, may hold values from -0.875 to 0.875
- b_attn_out: float32 [768], replicated, may hold values from -1.8 to 1.8
- norm2_gain: float32 [768], replicated, may hold values from 0.5 to 1.5
- norm2_bias: float32 [768], replicated, may hold values from -1.8 to 1.8
- w_in: bfloat16 [768, 3072], replicated, may hold values from -0.21875 to 0.21875
- b_in: float32 [3072], replicated, may hold values from -1.8 to 1.8
- w_out: bfloat16 [3072, 768], replicated, may hold values from -0.109375 to 0.109375
- b_out: float32 [768], replicated, may hold values from -1.8 to 1.8
- cotangent: bfloat16 [8192, 768], P(('dp', 'table')), may hold values from -6 to 6
Outputs:
- mixed: bfloat16 [8192, 768], P(('dp', 'table'))
- knowledge_grad: float32 [5, 4608, 768], P(None, ('dp', 'table'))
- expr_table_grad: float32 [128, 768], replicated
- norm1_gain_grad: float32 [768], replicated
- norm1_bias_grad: float32 [768], replicated
- w_query_grad: float32 [768, 768], replicated
- b_query_grad: float32 [768], replicated
- w_key_grad: float32 [768, 768], replicated
- w_value_grad: float32 [768, 768], replicated
- b_value_grad: float32 [768], replicated
- w_attn_out_grad: float32 [768, 768], replicated
- b_attn_out_grad: float32 [768], replicated
- norm2_gain_grad: float32 [768], replicated
- norm2_bias_grad: float32 [768], replicated
- w_in_grad: float32 [768, 3072], replicated
- b_in_grad: float32 [3072], replicated
- w_out_grad: float32 [3072, 768], replicated
- b_out_grad: float32 [768], replicated
Inputs may be any that keep to these rules, and one draw needn't show every extreme that they name: `gene_owner`: within the rows of one device no owner index is named by more than 16 rows, and in every draw some device names some owner exactly 16 times. `cell_lengths`: the 8 entries of one device sum to at most 256; the first is positive and zeros stand only after the positive ones. In every draw some device holds a single cell of 256 tokens.
All inputs are finite; a program needn't handle non-finite values.
Results may differ from a plain program's by a relative error of at most 0.012.
Values may be sent and summed in bfloat16 or wider, within the bound.
A program may use at most 192 MiB of HBM per device.

v0:
```python
import jax
import jax.numpy as jnp
from jax import lax
from jax.sharding import PartitionSpec as P

HEADS = 12
HEAD_DIM = 64
TABLES = 5
LAYER_EPS = 1e-05
GELU_SLOPE = 0.7978845608028654
GELU_CUBIC = 0.044715
MASKED = -1e30


def gelu_tanh(pre_act):
    return (
        0.5
        * pre_act
        * (1.0 + jnp.tanh(GELU_SLOPE * (pre_act + GELU_CUBIC * pre_act * pre_act * pre_act)))
    )


def layer_norm(inputs, gain, shift):
    average = jnp.mean(inputs, axis=-1, keepdims=True)
    centred = inputs - average
    spread = jnp.mean(centred * centred, axis=-1, keepdims=True)
    return centred * lax.rsqrt(spread + LAYER_EPS) * gain + shift


def cell_masks(lengths, count):
    cell_ends = jnp.cumsum(lengths)
    places = jnp.arange(count, dtype=jnp.int32)
    segment = jnp.sum((places[:, None] >= cell_ends[None, :]).astype(jnp.int32), axis=1)
    live_mask = (places < cell_ends[-1]).astype(jnp.float32)
    return (segment, live_mask)


def local(
    knowledge,
    expr_table,
    gene_owner,
    gene_row,
    expr_bin,
    cell_lengths,
    norm1_gain,
    norm1_bias,
    w_query,
    b_query,
    w_key,
    w_value,
    b_value,
    w_attn_out,
    b_attn_out,
    norm2_gain,
    norm2_bias,
    w_in,
    b_in,
    w_out,
    b_out,
    cotangent,
):
    devices = lax.axis_size(("dp", "table"))
    tok_count = cotangent.shape[0]
    model_width = cotangent.shape[1]
    table_rows = knowledge.shape[1]
    capacity = 2 * tok_count // devices
    owner_ids = gene_owner[:, 0]
    owner_hot = (owner_ids[:, None] == jnp.arange(devices, dtype=jnp.int32)[None, :]).astype(
        jnp.int32
    )
    running = jnp.cumsum(owner_hot, axis=0) - owner_hot
    slot_rank = jnp.sum(running * owner_hot, axis=1)
    send_slot = owner_ids * capacity + slot_rank
    outgoing = jnp.full((devices * capacity,), -1, jnp.int32).at[send_slot].set(gene_row)
    outgoing = outgoing.reshape(devices, capacity)
    arrived = lax.all_to_all(outgoing, ("dp", "table"), split_axis=0, concat_axis=0, tiled=True)
    slot_count = arrived.shape[1]
    flat_ids = arrived.reshape(-1)
    row_hot = (flat_ids[:, None] == jnp.arange(table_rows, dtype=jnp.int32)[None, :]).astype(
        jnp.bfloat16
    )
    picked = jnp.einsum(
        "sr,krd->skd", row_hot, knowledge, preferred_element_type=jnp.float32
    ).astype(jnp.bfloat16)
    returned_rows = lax.all_to_all(
        picked.reshape(devices, slot_count, TABLES * model_width),
        ("dp", "table"),
        split_axis=0,
        concat_axis=0,
        tiled=True,
    )
    owner_hot_rows = row_hot.reshape(devices, slot_count, table_rows)
    own_rows = returned_rows.reshape(devices * capacity, returned_rows.shape[2])[send_slot]
    gene_part = jnp.sum(own_rows.reshape(tok_count, TABLES, model_width), axis=1, dtype=jnp.float32)
    expr_hot = (
        expr_bin[:, None] == jnp.arange(expr_table.shape[0], dtype=jnp.int32)[None, :]
    ).astype(jnp.bfloat16)
    embedded = gene_part + jnp.dot(expr_hot, expr_table, preferred_element_type=jnp.float32)
    segment, live_mask = cell_masks(cell_lengths, tok_count)
    normed1, norm1_back = jax.vjp(layer_norm, embedded, norm1_gain, norm1_bias)
    attn_in = normed1.astype(jnp.bfloat16)
    query_rows = (jnp.dot(attn_in, w_query, preferred_element_type=jnp.float32) + b_query).astype(
        jnp.bfloat16
    )
    key_rows = jnp.dot(attn_in, w_key, preferred_element_type=jnp.float32).astype(jnp.bfloat16)
    value_rows = (jnp.dot(attn_in, w_value, preferred_element_type=jnp.float32) + b_value).astype(
        jnp.bfloat16
    )
    block_rows = min(512, tok_count)
    block_count = tok_count // block_rows
    score_scale = HEAD_DIM ** (-0.5)
    key_heads = key_rows.reshape(tok_count, HEADS, HEAD_DIM)
    value_heads = value_rows.reshape(tok_count, HEADS, HEAD_DIM)
    query_blocks = query_rows.reshape(block_count, block_rows, HEADS, HEAD_DIM)
    segment_blocks = segment.reshape(block_count, block_rows)

    def block_scores(query_part, segment_part):
        scores = (
            jnp.einsum("qhd,khd->hqk", query_part, key_heads, preferred_element_type=jnp.float32)
            * score_scale
        )
        same_cell = segment_part[:, None] == segment[None, :]
        return jnp.where(same_cell[None], scores, MASKED)

    def attend_forward(inputs):
        query_part, segment_part = inputs
        scores = block_scores(query_part, segment_part)
        row_max = jnp.max(scores, axis=-1, keepdims=True)
        exp_scores = jnp.exp(scores - row_max)
        row_total = jnp.sum(exp_scores, axis=-1, keepdims=True)
        attn_probs = (exp_scores / row_total).astype(jnp.bfloat16)
        context_part = jnp.einsum(
            "hqk,khd->qhd", attn_probs, value_heads, preferred_element_type=jnp.float32
        )
        return (context_part.astype(jnp.bfloat16), row_max + jnp.log(row_total))

    context_blocks, log_totals = lax.map(attend_forward, (query_blocks, segment_blocks))
    context = context_blocks.reshape(tok_count, model_width)
    attended = jnp.dot(context, w_attn_out, preferred_element_type=jnp.float32) + b_attn_out
    hidden1 = embedded + attended
    normed2, norm2_back = jax.vjp(layer_norm, hidden1, norm2_gain, norm2_bias)
    ffn_in = normed2.astype(jnp.bfloat16)
    pre_act = jnp.dot(ffn_in, w_in, preferred_element_type=jnp.float32) + b_in
    activated, gelu_back = jax.vjp(gelu_tanh, pre_act)
    act_low = activated.astype(jnp.bfloat16)
    hidden2 = hidden1 + jnp.dot(act_low, w_out, preferred_element_type=jnp.float32) + b_out
    mixed = (hidden2 * live_mask[:, None]).astype(jnp.bfloat16)
    grad_hidden2 = cotangent.astype(jnp.float32) * live_mask[:, None]
    grad_ffn = grad_hidden2.astype(jnp.bfloat16)
    b_out_grad = jnp.sum(grad_ffn, axis=0, dtype=jnp.float32)
    w_out_grad = jnp.einsum("tf,td->fd", act_low, grad_ffn, preferred_element_type=jnp.float32)
    grad_act = jnp.einsum("td,fd->tf", grad_ffn, w_out, preferred_element_type=jnp.float32)
    grad_pre = gelu_back(grad_act)[0].astype(jnp.bfloat16)
    b_in_grad = jnp.sum(grad_pre, axis=0, dtype=jnp.float32)
    w_in_grad = jnp.einsum("td,tf->df", ffn_in, grad_pre, preferred_element_type=jnp.float32)
    grad_normed2 = jnp.einsum("tf,df->td", grad_pre, w_in, preferred_element_type=jnp.float32)
    grad_from2, norm2_gain_grad, norm2_bias_grad = norm2_back(grad_normed2)
    grad_hidden1 = grad_hidden2 + grad_from2
    grad_attn = grad_hidden1.astype(jnp.bfloat16)
    b_attn_out_grad = jnp.sum(grad_attn, axis=0, dtype=jnp.float32)
    w_attn_out_grad = jnp.einsum(
        "td,te->de", context, grad_attn, preferred_element_type=jnp.float32
    )
    grad_context = jnp.einsum(
        "te,de->td", grad_attn, w_attn_out, preferred_element_type=jnp.float32
    ).astype(jnp.bfloat16)
    grad_blocks = grad_context.reshape(block_count, block_rows, HEADS, HEAD_DIM)

    def attend_backward(carry, inputs):
        key_sum, value_sum = carry
        query_part, segment_part, log_part, grad_part = inputs
        scores = block_scores(query_part, segment_part)
        attn_probs = jnp.exp(scores - log_part)
        grad_probs = jnp.einsum(
            "qhd,khd->hqk", grad_part, value_heads, preferred_element_type=jnp.float32
        )
        value_sum = value_sum + jnp.einsum(
            "hqk,qhd->khd",
            attn_probs.astype(jnp.bfloat16),
            grad_part,
            preferred_element_type=jnp.float32,
        )
        grad_scores = attn_probs * (
            grad_probs - jnp.sum(attn_probs * grad_probs, axis=-1, keepdims=True)
        )
        grad_scores = grad_scores.astype(jnp.bfloat16)
        grad_query_part = (
            jnp.einsum("hqk,khd->qhd", grad_scores, key_heads, preferred_element_type=jnp.float32)
            * score_scale
        )
        key_sum = (
            key_sum
            + jnp.einsum(
                "hqk,qhd->khd", grad_scores, query_part, preferred_element_type=jnp.float32
            )
            * score_scale
        )
        return ((key_sum, value_sum), grad_query_part.astype(jnp.bfloat16))

    zero_heads = jnp.zeros((tok_count, HEADS, HEAD_DIM), jnp.float32)
    (key_sum, value_sum), grad_query_blocks = lax.scan(
        attend_backward,
        (zero_heads, zero_heads),
        (query_blocks, segment_blocks, log_totals, grad_blocks),
    )
    grad_query = grad_query_blocks.reshape(tok_count, model_width)
    grad_keys = key_sum.reshape(tok_count, model_width).astype(jnp.bfloat16)
    grad_values = value_sum.reshape(tok_count, model_width).astype(jnp.bfloat16)
    w_query_grad = jnp.einsum("td,te->de", attn_in, grad_query, preferred_element_type=jnp.float32)
    b_query_grad = jnp.sum(grad_query, axis=0, dtype=jnp.float32)
    w_key_grad = jnp.einsum("td,te->de", attn_in, grad_keys, preferred_element_type=jnp.float32)
    w_value_grad = jnp.einsum("td,te->de", attn_in, grad_values, preferred_element_type=jnp.float32)
    b_value_grad = jnp.sum(grad_values, axis=0, dtype=jnp.float32)
    grad_normed1 = jnp.einsum("te,de->td", grad_query, w_query, preferred_element_type=jnp.float32)
    grad_normed1 = grad_normed1 + jnp.einsum(
        "te,de->td", grad_keys, w_key, preferred_element_type=jnp.float32
    )
    grad_normed1 = grad_normed1 + jnp.einsum(
        "te,de->td", grad_values, w_value, preferred_element_type=jnp.float32
    )
    grad_from1, norm1_gain_grad, norm1_bias_grad = norm1_back(grad_normed1)
    grad_embedded = (grad_hidden1 + grad_from1).astype(jnp.bfloat16)
    expr_table_grad = jnp.einsum(
        "tb,td->bd", expr_hot, grad_embedded, preferred_element_type=jnp.float32
    )
    outgoing_grads = (
        jnp.zeros((devices * capacity, model_width), jnp.bfloat16).at[send_slot].set(grad_embedded)
    )
    arrived_grads = lax.all_to_all(
        outgoing_grads.reshape(devices, capacity, model_width),
        ("dp", "table"),
        split_axis=0,
        concat_axis=0,
        tiled=True,
    )
    table_grad = jnp.einsum(
        "gsr,gsd->rd", owner_hot_rows, arrived_grads, preferred_element_type=jnp.float32
    )
    knowledge_grad = jnp.broadcast_to(table_grad[None], (TABLES, table_rows, model_width))
    summed = lax.psum(
        (
            w_in_grad,
            b_in_grad,
            w_out_grad,
            b_out_grad,
            norm2_gain_grad,
            norm2_bias_grad,
            norm1_gain_grad,
            norm1_bias_grad,
            w_query_grad,
            b_query_grad,
            w_key_grad,
            w_value_grad,
            b_value_grad,
            w_attn_out_grad,
            b_attn_out_grad,
            expr_table_grad,
        ),
        ("dp", "table"),
    )
    ffn_terms = summed[:6]
    attn_terms = summed[6:]
    return (
        mixed,
        knowledge_grad,
        attn_terms[9],
        attn_terms[0],
        attn_terms[1],
        attn_terms[2],
        attn_terms[3],
        attn_terms[4],
        attn_terms[5],
        attn_terms[6],
        attn_terms[7],
        attn_terms[8],
        ffn_terms[4],
        ffn_terms[5],
        ffn_terms[0],
        ffn_terms[1],
        ffn_terms[2],
        ffn_terms[3],
    )


def solution(mesh):
    in_specs = (
        P(None, ("dp", "table"), None),
        P(),
        P(("dp", "table"), None),
        P(("dp", "table")),
        P(("dp", "table")),
        P(("dp", "table")),
        P(),
        P(),
        P(),
        P(),
        P(),
        P(),
        P(),
        P(),
        P(),
        P(),
        P(),
        P(),
        P(),
        P(),
        P(),
        P(("dp", "table"), None),
    )
    out_specs = (
        P(("dp", "table"), None),
        P(None, ("dp", "table"), None),
        P(),
        P(),
        P(),
        P(),
        P(),
        P(),
        P(),
        P(),
        P(),
        P(),
        P(),
        P(),
        P(),
        P(),
        P(),
        P(),
    )
    return jax.shard_map(local, mesh=mesh, in_specs=in_specs, out_specs=out_specs, check_vma=False)
```

profile of v0, /device:TPU:0, one launch (start us, length us, event | category | flops | bytes accessed | tf_op | source)
XLA Modules:
  0.0 698.4 jit_solution(7294578656699365862)
XLA Ops:
  11.9 14.3 %all_to_all.19 = s32[32,1,16]{2,1,0:T(1,128)S(1)} all-to-all(s32[32,1,16]{2,1,0:T(1,128)S(1)} %bitcast.118), channel_id=1, replica_groups=mesh['dp'=8,'table'=4] {'dp','table'}, dimensions={0} | all-to-all | bytes 4096 | tf_op jit(solution)/shard_map/all_to_all | solution.py:76
  27.5 2.6 convolution_convert_fusion
  30.0 5.2 copy.82
  35.2 9.8 %reshape.233 = bf16[32,16,3840]{2,1,0:T(8,128)(2,1)} reshape(bf16[512,5,768]{2,1,0:T(8,128)(2,1)} %copy.82) | data formatting | bytes 7864320 | tf_op jit(solution)/shard_map/reshape | solution.py:86
  45.0 3.7 all-to-all-start.1
  51.6 84.0 %all-to-all-done.1 = bf16[32,16,3840]{2,1,0:T(8,128)(2,1)} async-done(((bf16[32,16,3840]{2,1,0:T(8,128)(2,1)}), bf16[32,16,3840]{2,1,0:T(8,128)(2,1)}, u32[]{:S(2)}, u32[]{:S(2)}) %all-to-all-start.1) | async-done | bytes 3932192 | tf_op jit(solution)/shard_map/all_to_all | solution.py:85
  135.5 6.4 gather_fusion
  141.9 3.2 copy.83
  145.1 2.5 reduce_sum.240
  161.7 5.4 convert_reduce_fusion
  167.1 2.3 multiply_reduce_fusion.1
  176.5 3.4 convert_reduce_fusion.3
  183.6 1.9 fusion.58
  185.6 6.0 fusion.44
  191.6 5.3 fusion.50
  197.0 1.9 fusion.60
  198.9 1.9 fusion.59
  204.3 2.7 scatter_custom_fusion.1
  207.0 5.4 all-to-all-start.2
  212.7 50.9 %all-reduce = (f32[768]{0:T(1024)}, f32[768]{0:T(1024)}, f32[768]{0:T(1024)}, f32[768]{0:T(1024)}, f32[768]{0:T(1024)}, /*index=5*/f32[768]{0:T(1024)}, f32[768]{0:T(1024)}, f32[3072]{0:T(1024)}, f32[768]{0:T(1024)}) all-reduce(f32[768]{0:T(1024)S(1)} %get-tuple-element.77, ...), channel_id=1, replica_groups=mesh['dp'=8,'table'=4] {'dp','table'}, use_global_device_ids=true, to_apply=%region_21.22 | all-reduce | flops 9216 | bytes 73728 | tf_op jit(solution)/shard_map/psum | solution.py:240
  263.5 6.3 fusion.23
  270.3 396.6 %all-reduce.4.cloned.1.call-done = (f32[128,768]{1,0:T(8,128)}, f32[768,768]{1,0:T(8,128)}, f32[768,768]{1,0:T(8,128)}, f32[768,768]{1,0:T(8,128)}, f32[768,768]...) async-done(((f32[128,768]{1,0:T(8,128)}, f32[768,768]{1,0:T(8,128)}, f32[768,768]{1,0:T(8,128)}, f32[768,768]{1,0:T(8,128)}, f32[768,768]{1,0:T(8,128)}, ...) | async-done | bytes 28704784 | tf_op jit(solution)/shard_map/psum | solution.py:240
  678.3 9.3 %copy.115 = f32[768,3072]{1,0:T(8,128)} copy(f32[768,3072]{1,0:T(8,128)} %get-tuple-element.134) | data formatting | bytes 18874368
  687.6 3.7 copy.116
  (218 shorter events, 48.5 us)
Async XLA Ops:
  7.2 144.7 %copy-start = (bf16[768,768]{1,0:T(8,128)(2,1)S(1)}, bf16[768,768]{1,0:T(8,128)(2,1)}, u32[]{:S(2)}) copy-start(bf16[768,768]{1,0:T(8,128)(2,1)} %param.33) | copy-start | bytes 3538948
  10.3 40.5 %copy-start.57 = (s32[256,1]{0,1:T(1,128)}, s32[256,1]{0,1:T(1,128)S(1)}, u32[]{:S(2)}) copy-start(s32[256,1]{0,1:T(1,128)S(1)} %compare_select_fusion) | copy-start | bytes 3076
  26.2 9.1 %copy-start.26 = (s32[32,1,16]{2,1,0:T(1,128)}, s32[32,1,16]{2,1,0:T(1,128)S(1)}, u32[]{:S(2)}) copy-start(s32[32,1,16]{2,1,0:T(1,128)S(1)} %all_to_all.19) | copy-start | bytes 6148
  45.0 90.5 %all-to-all-start.1 = ((bf16[32,16,3840]{2,1,0:T(8,128)(2,1)}), bf16[32,16,3840]{2,1,0:T(8,128)(2,1)}, u32[]{:S(2)}, u32[]{:S(2)}) async-start(bf16[32,16,3840]{2,1,0:T(8,128)(2,1)} %reshape.233), calls=%async_computation.1 | async-start | bytes 7864320 | tf_op jit(solution)/shard_map/all_to_all | solution.py:85
  48.7 618.2 %all-reduce.4.cloned.1.call-start = ((), (), s32[]{:S(2)}) async-start(), calls=%async_computation.3 | async-start | bytes 57409536 | tf_op jit(solution)/shard_map/psum | solution.py:240
  149.8 6.1 copy-start.11
  159.7 9.7 %copy-start.37 = (f32[256]{0:T(256)}, f32[256]{0:T(256)S(1)}, u32[]{:S(2)}) copy-start(f32[256]{0:T(256)S(1)} %broadcast_multiply_fusion) | copy-start | bytes 3076
  160.0 9.4 %copy-start.43 = (f32[256]{0:T(256)}, f32[256]{0:T(256)S(1)}, u32[]{:S(2)}) copy-start(f32[256]{0:T(256)S(1)} %fusion.43) | copy-start | bytes 3076
  185.5 6.1 copy-start.23
  185.5 6.1 copy-start.29
  185.5 6.1 copy-start.31
  204.2 8.2 %copy-start.27 = (s32[32,1,16]{2,1,0:T(1,128)S(1)}, s32[32,1,16]{2,1,0:T(1,128)}, u32[]{:S(2)}) copy-start(s32[32,1,16]{2,1,0:T(1,128)} %copy-done.26) | copy-start | bytes 6148
  204.2 8.3 %copy-start.34 = (f32[12,64]{1,0:T(8,128)S(1)}, f32[12,64]{1,0:T(8,128)}, u32[]{:S(2)}) copy-start(f32[12,64]{1,0:T(8,128)} %get-tuple-element.116) | copy-start | bytes 9220
  204.2 8.4 %copy-start.41 = (f32[768]{0:T(1024)S(1)}, f32[768]{0:T(1024)}, u32[]{:S(2)}) copy-start(f32[768]{0:T(1024)} %get-tuple-element.97) | copy-start | bytes 9220
  204.2 8.4 %copy-start.42 = (f32[768]{0:T(1024)S(1)}, f32[768]{0:T(1024)}, u32[]{:S(2)}) copy-start(f32[768]{0:T(1024)} %get-tuple-element.103) | copy-start | bytes 9220
  204.2 8.4 %copy-start.45 = (f32[3072]{0:T(1024)S(1)}, f32[3072]{0:T(1024)}, u32[]{:S(2)}) copy-start(f32[3072]{0:T(1024)} %get-tuple-element.118) | copy-start | bytes 36868
  204.2 8.4 %copy-start.58 = (f32[768]{0:T(1024)S(1)}, f32[768]{0:T(1024)}, u32[]{:S(2)}) copy-start(f32[768]{0:T(1024)} %get-tuple-element.64) | copy-start | bytes 9220
  204.2 8.4 %copy-start.59 = (f32[768]{0:T(1024)S(1)}, f32[768]{0:T(1024)}, u32[]{:S(2)}) copy-start(f32[768]{0:T(1024)} %get-tuple-element.79) | copy-start | bytes 9220
  204.2 59.3 %copy-start.48 = (f32[256]{0:T(256)S(1)}, f32[256]{0:T(256)}, u32[]{:S(2)}) copy-start(f32[256]{0:T(256)} %compare_convert_fusion) | copy-start | bytes 3076
  204.3 59.3 %copy-start.63 = (f32[768]{0:T(1024)S(1)}, f32[768]{0:T(1024)}, u32[]{:S(2)}) copy-start(f32[768]{0:T(1024)} %param.42) | copy-start | bytes 9220
  207.0 62.8 %all-to-all-start.2 = ((bf16[32,16,768]{2,1,0:T(8,128)(2,1)}), bf16[32,16,768]{2,1,0:T(8,128)(2,1)S(1)}, u32[]{:S(2)}, u32[]{:S(2)}) async-start(bf16[32,16,768]{2,1,0:T(8,128)(2,1)} %bitcast.25), calls=%async_computation.2 | async-start | bytes 1572864 | tf_op jit(solution)/shard_map/all_to_all | solution.py:229
  676.9 10.7 %slice-start = ((s8[9437184]{0:T(1024)(128)(4,1)}), s8[4194304]{0:T(1024)(128)(4,1)S(1)}, s32[]{:S(2)}) async-start(s8[9437184]{0:T(1024)(128)(4,1)} %bitcast.99), calls=%async_computation.4 | async-start | bytes 8388608
  678.3 9.3 %slice-start.1 = ((s8[9437184]{0:T(1024)(128)(4,1)}), s8[4194304]{0:T(1024)(128)(4,1)S(1)}, s32[]{:S(2)}) async-start(s8[9437184]{0:T(1024)(128)(4,1)} %bitcast.99), calls=%async_computation.5 | async-start | bytes 8388608
  678.3 9.3 %slice-start.2 = ((s8[9437184]{0:T(1024)(128)(4,1)}), s8[1048576]{0:T(1024)(128)(4,1)S(1)}, s32[]{:S(2)}) async-start(s8[9437184]{0:T(1024)(128)(4,1)} %bitcast.99), calls=%async_computation.6 | async-start | bytes 2097152
  (51 other events, 125.3 us)
Sparse Core Ops, SparseCore 0:
  204.4 462.5 all-reduce.3
where the time goes:
time: 707 us; the launch traced here: 698 us
  waiting for transfers between devices  481 us (68%)
  blocking collectives  65.2 us (9%)
  local copies, waits for them, and re-layouts  62.5 us (9%)
  matrix products  54.1 us (8%)
  between operations  15.1 us (2%)
  other arithmetic  11.8 us (2%)
  starting transfers between devices  9.12 us (1%)
    psum x1, waiting for transfers between devices, local(): lax.psum((w_in_grad, b_in_grad, w_out_grad, b_out_grad, norm2_gain_grad,...  397 us
    all_to_all x1, waiting for transfers between devices, local(): lax.all_to_all(picked.reshape(devices, slot_count, TABLES * model_width),...  84 us
    psum x1, blocking collectives, local(): lax.psum((w_in_grad, b_in_grad, w_out_grad, b_out_grad, norm2_gain_grad,...  50.9 us
    unnamed x151, local copies, waits for them, and re-layouts  26.8 us
    all_to_all x1, blocking collectives, local(): lax.all_to_all(outgoing, ('dp', 'table'), split_axis=0, concat_axis=0, ti...  14.3 us
  transfers between devices with their start and end apart: 3, of which 2 were waited for; matrix products, arithmetic and copies ran while one was open for 2% of the time, Pallas kernels for 0%

commit v1 on v0

--- a/solution.py
+++ b/solution.py
@@ -238,25 +238,28 @@
     )
     knowledge_grad = jnp.broadcast_to(table_grad[None], (TABLES, table_rows, model_width))
     summed = lax.psum(
-        (
-            w_in_grad,
-            b_in_grad,
-            w_out_grad,
-            b_out_grad,
-            norm2_gain_grad,
-            norm2_bias_grad,
-            norm1_gain_grad,
-            norm1_bias_grad,
-            w_query_grad,
-            b_query_grad,
-            w_key_grad,
-            w_value_grad,
-            b_value_grad,
-            w_attn_out_grad,
-            b_attn_out_grad,
-            expr_table_grad,
+        lax.psum(
+            (
+                w_in_grad,
+                b_in_grad,
+                w_out_grad,
+                b_out_grad,
+                norm2_gain_grad,
+                norm2_bias_grad,
+                norm1_gain_grad,
+                norm1_bias_grad,
+                w_query_grad,
+                b_query_grad,
+                w_key_grad,
+                w_value_grad,
+                b_value_grad,
+                w_attn_out_grad,
+                b_attn_out_grad,
+                expr_table_grad,
+            ),
+            "table",
         ),
-        ("dp", "table"),
+        "dp",
     )
     ffn_terms = summed[:6]
     attn_terms = summed[6:]

time: 707 us -> 1570 us (2.22)
  waiting for transfers between devices: 481 us -> 1330 us
    psum x1, waiting for transfers between devices: 397 us -> 955 us  [local(): lax.psum((w_in_grad, b_in_grad, w_out_grad, b_out_grad, norm2_gain_grad,...]
    psum x0 -> x1, waiting for transfers between devices: none -> 294 us  [local(): lax.psum(lax.psum((w_in_grad, b_in_grad, w_out_grad, b_out_grad, norm2_ga...]
    psum x0 -> x1, blocking collectives: none -> 25.6 us  [local(): lax.psum(lax.psum((w_in_grad, b_in_grad, w_out_grad, b_out_grad, norm2_ga...]
    psum x1, blocking collectives: 50.9 us -> 29.7 us  [local(): lax.psum((w_in_grad, b_in_grad, w_out_grad, b_out_grad, norm2_gain_grad,...]
  transfers between devices with their start and end apart: 3 -> 4, of which waited for: 2 -> 3; matrix products, arithmetic and copies ran while one was open for 2% -> 1% of each run, Pallas kernels for 0% -> 0%
where the time goes in v1:
time: 1570 us; the launch traced here: 1560 us
  waiting for transfers between devices  1330 us (85%)
  blocking collectives  69.5 us (4%)
  local copies, waits for them, and re-layouts  65.7 us (4%)
  matrix products  54 us (3%)
    psum x1, waiting for transfers between devices, local(): lax.psum((w_in_grad, b_in_grad, w_out_grad, b_out_grad, norm2_gain_grad,...  955 us
    psum x1, waiting for transfers between devices, local(): lax.psum(lax.psum((w_in_grad, b_in_grad, w_out_grad, b_out_grad, norm2_ga...  294 us
    all_to_all x1, waiting for transfers between devices, local(): lax.all_to_all(picked.reshape(devices, slot_count, TABLES * model_width),...  83.9 us
  transfers between devices with their start and end apart: 4, of which 3 were waited for; matrix products, arithmetic and copies ran while one was open for 1% of the time, Pallas kernels for 0%

profile of v1, /device:TPU:0, one launch (start us, length us, event | category | flops | bytes accessed | tf_op | source)
XLA Modules:
  0.0 1556.8 jit_solution(17918385169577667618)
XLA Ops:
  11.9 14.3 all_to_all.19
  27.5 2.6 convolution_convert_fusion
  30.0 5.2 copy.82
  35.2 9.8 reshape.233
  45.0 3.7 all-to-all-start.1
  51.6 83.9 %all-to-all-done.1 = bf16[32,16,3840]{2,1,0:T(8,128)(2,1)} async-done(((bf16[32,16,3840]{2,1,0:T(8,128)(2,1)}), bf16[32,16,3840]{2,1,0:T(8,128)(2,1)}, u32[]{:S(2)}, u32[]{:S(2)}) %all-to-all-start.1) | async-done | bytes 3932192 | tf_op jit(solution)/shard_map/all_to_all | solution.py:85
  135.5 7.6 gather_fusion
  143.2 4.6 copy.83
  147.8 2.5 reduce_sum.240
  164.9 5.4 convert_reduce_fusion
  170.3 2.3 multiply_reduce_fusion.1
  179.8 3.4 convert_reduce_fusion.3
  186.9 1.9 fusion.58
  188.8 6.0 fusion.44
  194.9 5.3 fusion.50
  207.5 955.4 %all-reduce.9.cloned.1.call-done = (f32[128,768]{1,0:T(8,128)}, f32[768,768]{1,0:T(8,128)}, f32[768,768]{1,0:T(8,128)}, f32[768,768]{1,0:T(8,128)}, f32[768,768]...) async-done(((f32[128,768]{1,0:T(8,128)}, f32[768,768]{1,0:T(8,128)}, f32[768,768]{1,0:T(8,128)}, f32[768,768]{1,0:T(8,128)}, f32[768,768]{1,0:T(8,128)}, ...) | async-done | bytes 28704784 | tf_op jit(solution)/shard_map/psum | solution.py:241
  1163.0 2.7 scatter_custom_fusion.1
  1165.7 3.8 all-to-all-start.2
  1169.8 29.7 %all-reduce.2 = (f32[768]{0:T(1024)S(1)}, f32[768]{0:T(1024)S(1)}, f32[768]{0:T(1024)S(1)}, f32[768]{0:T(1024)S(1)}, f32[768]{0:T(1024)S(1)}, /*index=5*/f32[768...) all-reduce(f32[768]{0:T(1024)S(1)} %get-tuple-element.77, ...), channel_id=1, replica_groups=mesh['dp'=8,'table'=4] {'table'}, use_global_device_ids=true, to_apply=%region_22.23 | all-reduce | flops 9216 | bytes 73728 | tf_op jit(solution)/shard_map/psum | solution.py:241
  1199.5 25.6 %all-reduce = (f32[768]{0:T(1024)}, f32[768]{0:T(1024)}, f32[768]{0:T(1024)}, f32[768]{0:T(1024)}, f32[768]{0:T(1024)}, /*index=5*/f32[768]{0:T(1024)}, f32[768]{0:T(1024)}, f32[3072]{0:T(1024)}, f32[768]{0:T(1024)}) all-reduce(f32[768]{0:T(1024)S(1)} %get-tuple-element.97, ...), channel_id=1, replica_groups=mesh['dp'=8,'table'=4] {'dp'}, use_global_device_ids=true, to_apply=%region_23.24 | all-reduce | flops 9216 | bytes 73728 | tf_op jit(solution)/shard_map/psum | solution.py:240
  1225.1 6.1 fusion.23
  1231.8 293.6 %all-reduce.7.cloned.1.call-done = (f32[128,768]{1,0:T(8,128)}, f32[768,768]{1,0:T(8,128)}, f32[768,768]{1,0:T(8,128)}, f32[768,768]{1,0:T(8,128)}, f32[768,768]...) async-done(((f32[128,768]{1,0:T(8,128)}, f32[768,768]{1,0:T(8,128)}, f32[768,768]{1,0:T(8,128)}, f32[768,768]{1,0:T(8,128)}, f32[768,768]{1,0:T(8,128)}, ...) | async-done | bytes 28704784 | tf_op jit(solution)/shard_map/psum | solution.py:240
  1536.6 9.3 copy.122
  1546.0 3.7 copy.123
  (222 shorter events, 53.0 us)
Async XLA Ops:
  7.2 148.0 %copy-start = (bf16[768,768]{1,0:T(8,128)(2,1)S(1)}, bf16[768,768]{1,0:T(8,128)(2,1)}, u32[]{:S(2)}) copy-start(bf16[768,768]{1,0:T(8,128)(2,1)} %param.33) | copy-start | bytes 3538948
  10.3 40.5 %copy-start.57 = (s32[256,1]{0,1:T(1,128)}, s32[256,1]{0,1:T(1,128)S(1)}, u32[]{:S(2)}) copy-start(s32[256,1]{0,1:T(1,128)S(1)} %compare_select_fusion) | copy-start | bytes 3076
  26.2 9.1 copy-start.26
  45.0 90.5 %all-to-all-start.1 = ((bf16[32,16,3840]{2,1,0:T(8,128)(2,1)}), bf16[32,16,3840]{2,1,0:T(8,128)(2,1)}, u32[]{:S(2)}, u32[]{:S(2)}) async-start(bf16[32,16,3840]{2,1,0:T(8,128)(2,1)} %reshape.233), calls=%async_computation.1 | async-start | bytes 7864320 | tf_op jit(solution)/shard_map/all_to_all | solution.py:85
  48.7 1114.2 %all-reduce.9.cloned.1.call-start = ((), (), s32[]{:S(2)}) async-start(), calls=%async_computation.4 | async-start | bytes 57409536 | tf_op jit(solution)/shard_map/psum | solution.py:241
  153.1 6.1 copy-start.11
  163.0 9.7 copy-start.37
  163.3 9.4 copy-start.43
  188.8 6.1 copy-start.23
  188.8 6.1 copy-start.29
  207.5 1317.8 %all-reduce.7.cloned.1.call-start = ((), (), s32[]{:S(2)}) async-start(), calls=%async_computation.3 | async-start | bytes 57409536 | tf_op jit(solution)/shard_map/psum | solution.py:240
  1162.9 6.6 copy-start.27
  1162.9 6.7 copy-start.34
  1162.9 6.9 copy-start.41
  1162.9 6.9 copy-start.42
  1162.9 6.9 copy-start.45
  1163.0 6.8 copy-start.58
  1163.0 6.8 copy-start.59
  1163.0 62.1 %copy-start.48 = (f32[256]{0:T(256)S(1)}, f32[256]{0:T(256)}, u32[]{:S(2)}) copy-start(f32[256]{0:T(256)} %compare_convert_fusion) | copy-start | bytes 3076
  1163.0 62.1 %copy-start.63 = (f32[768]{0:T(1024)S(1)}, f32[768]{0:T(1024)}, u32[]{:S(2)}) copy-start(f32[768]{0:T(1024)} %param.42) | copy-start | bytes 9220
  1165.7 65.5 %all-to-all-start.2 = ((bf16[32,16,768]{2,1,0:T(8,128)(2,1)}), bf16[32,16,768]{2,1,0:T(8,128)(2,1)S(1)}, u32[]{:S(2)}, u32[]{:S(2)}) async-start(bf16[32,16,768]{2,1,0:T(8,128)(2,1)} %bitcast.25), calls=%async_computation.2 | async-start | bytes 1572864 | tf_op jit(solution)/shard_map/all_to_all | solution.py:229
  1535.2 10.7 slice-start
  1536.6 9.3 slice-start.1
  1536.6 9.3 slice-start.2
  (52 other events, 134.0 us)
Sparse Core Ops, SparseCore 0:
  207.6 955.2 all-reduce.8
  1168.1 357.1 all-reduce.6
